TPU v7x, 32 devices: a whole 2x2x4 slice. The times are simulated.
32 devices in a mesh: groups: 2 (over y), tm: 8 (over z, x), space: 2 (over core).
Axes of the slice: x: 2, y: 2, z: 4, core: 2. Of those that a mesh axis runs over, the one named last changes fastest.
Arguments:
- iterate: float32 [16, 64, 512], P(('groups', 'tm'), None, 'space'), parts along dimension 0, may hold values from -6 to 6
- forcing: bfloat16 [64, 64, 512], P(('groups', 'tm'), None, 'space'), parts along dimension 0, may hold values from -6 to 6
- initial: float32 [128, 512], P('groups', 'space'), parts along dimension 0, may hold values from -6 to 6
- self_block: float32 [64, 64], replicated, may hold values from -0.5 to 1
- face_blocks: float32 [6, 64, 64], replicated, may hold values from -0.075 to 0.075
- element_gain: float32 [512], P('space'), may hold values from 0.5 to 1.5
- neighbors: int32 [6, 512], P(None, 'space'), may hold values from 0 to 319, as said below
- face_mask: int32 [6, 512], P(None, 'space'), may hold values from 0 to 1
- coarse_decay: bfloat16 [16, 64, 512], P(('groups', 'tm'), None, 'space'), parts along dimension 0, may hold values from 0 to 1
Outputs:
- fine_states: float32 [64, 64, 512], P(('groups', 'tm'), None, 'space'), parts along dimension 0
There are 2 independent parts, one for each index of `groups`. A program takes and returns all parts, laid end to end along the dimension named above; an argument that names none is the same for every part. Nothing has to cross between parts.
Inputs may be any that keep to these rules, and one draw needn't show every extreme that they name: `neighbors`: for element j of space block s, a value v < 256 names element s * 256 + v of the same block; a value v >= 256 names element (1 - s) * 256 + v - 64 of the other block, which is one of that block's last 64 elements; where face_mask is 0 the value is 0.
All inputs are finite; a program needn't handle non-finite values.
Results may differ from a plain program's by a relative error of at most 0.0003.
Values sent between devices are 32-bit elements; how exact they have to be, the bound alone decides.
A program may use at most 64 MiB of HBM per device.

v0:
```python
import jax
import jax.numpy as jnp
from jax import lax
from jax.sharding import PartitionSpec as P

CF = 4
BND = 64


highest = lax.Precision.HIGHEST


def swapped(block, axis, apart):
    count = lax.axis_size(axis)
    route = []
    for low in range(count):
        high = low | 1 << apart
        if high != low and high < count:
            route += [(low, high), (high, low)]
    return lax.ppermute(block, axis, route)


def from_behind(array, axis, by):
    count = lax.axis_size(axis)
    pairs = [(i, i + by) for i in range(count) if 0 <= i + by < count]
    return lax.ppermute(array, axis, pairs)


def carried_in(part, axis, combine, identity):
    place = lax.axis_index(axis)
    gathered = jax.tree.map(lambda a: lax.all_gather(a, axis), part)
    state = jax.tree.map(lambda a, e: jnp.zeros_like(a) + jnp.asarray(e, a.dtype), part, identity)

    def one(lap, state):
        return combine(
            state, jax.tree.map(lambda a: lax.dynamic_index_in_dim(a, lap, 0, False), gathered)
        )

    return lax.fori_loop(0, place, one, state)


def propagate(state_field, self_block, face_blocks, element_gain, neighbors, weights):
    elements = state_field.shape[1]
    partner = swapped(state_field[:, elements - BND :], "space", 0)
    extended = jnp.concatenate([state_field, partner], axis=1)
    nearby = jnp.take(extended, neighbors, axis=1) * weights[None]
    summed = jnp.dot(self_block, state_field, precision=highest, preferred_element_type=jnp.float32)
    summed = summed + jnp.einsum(
        "fij,jfe->ie", face_blocks, nearby, precision=highest, preferred_element_type=jnp.float32
    )
    return summed * element_gain[None]


def compose(earlier, later):
    return (earlier[0] * later[0], later[0] * earlier[1] + later[1])


def local(
    iterate,
    forcing,
    initial,
    self_block,
    face_blocks,
    element_gain,
    neighbors,
    face_mask,
    coarse_decay,
):
    weights = face_mask.astype(jnp.float32)
    sources = forcing.astype(jnp.float32)
    c_point = iterate[0]
    time_index = lax.axis_index("tm")
    previous = from_behind(c_point, "tm", 1)
    incoming_c = jnp.where(time_index == 0, initial, previous)

    def advance(state_field):
        return propagate(state_field, self_block, face_blocks, element_gain, neighbors, weights)

    current = incoming_c
    for section in range(CF):
        current = advance(current) + sources[section]
    residual = current - c_point
    damping_ratio = coarse_decay[0].astype(jnp.float32)
    prefix = carried_in(
        (damping_ratio, residual),
        "tm",
        compose,
        (jnp.ones_like(damping_ratio), jnp.zeros_like(residual)),
    )
    incoming = prefix[1]
    corrected = c_point + (damping_ratio * incoming + residual)
    current = incoming_c + incoming
    outputs = []
    for section in range(CF - 1):
        current = advance(current) + sources[section]
        outputs.append(current)
    outputs.append(corrected)
    return jnp.stack(outputs, axis=0)


def solution(mesh):
    placed = (
        P(("groups", "tm"), None, "space"),
        P(("groups", "tm"), None, "space"),
        P("groups", "space"),
        P(),
        P(),
        P("space"),
        P(None, "space"),
        P(None, "space"),
        P(("groups", "tm"), None, "space"),
    )
    return jax.shard_map(
        local,
        mesh=mesh,
        in_specs=placed,
        out_specs=P(("groups", "tm"), None, "space"),
        check_vma=False,
    )
```

profile of v0, /device:TPU:0, one launch (start us, length us, event | category | flops | bytes accessed | tf_op | source)
XLA Modules:
  0.0 106.6 jit_solution(15683257508303525638)
XLA Ops:
  0.0 5.0 %collective-permute-start = (f32[64,256]{1,0:T(8,128)}, f32[64,256]{1,0:T(8,128)S(1)}, u32[]{:S(2)}, u32[]{:S(2)}) collective-permute-start(f32[64,256]{1,0:T(8,128)} %bitcast.155), channel_id=1, source_target_pairs={{0,2},{2,4},{4,6},{6,8},{8,10},{10,12},{12,14},{1,3},{3,5},{5,7},{... | collective-permute-start | bytes 196616 | tf_op jit(solution)/shard_map/ppermute | solution.py:26
  5.0 0.7 compare_select_fusion
  5.7 1.5 %collective-permute-done = f32[64,256]{1,0:T(8,128)S(1)} collective-permute-done((f32[64,256]{1,0:T(8,128)}, f32[64,256]{1,0:T(8,128)S(1)}, u32[]{:S(2)}, u32[]{:S(2)}) %collective-permute-start) | collective-permute-done | bytes 65568 | tf_op jit(solution)/shard_map/ppermute | solution.py:26
  7.2 0.8 broadcast_select_fusion
  8.0 0.1 slice.61
  8.2 0.7 copy-done.7
  8.8 0.5 collective-permute-done.1
  9.3 0.1 copy.24
  9.5 2.6 %gather_fusion = f32[1536,64]{1,0:T(8,128)S(1)} fusion(f32[64,320]{0,1:T(8,128)S(1)} %copy.24, s32[2048]{0:T(1024)S(1)} %pad_clamp_fusion), kind=kCustom, calls=%fused_computation.clone | custom fusion | bytes 792576 | tf_op jit(solution)/shard_map/jit(_take)/gather | solution.py:46
  12.1 0.2 copy.25
  12.3 0.4 convolution_bitcast_fusion.6
  12.8 0.3 copy-done.1
  13.1 0.2 fusion.21
  13.3 0.1 slice.63
  13.4 0.2 collective-permute-start.2
  13.5 1.0 collective-permute-done.2
  14.6 0.1 copy.26
  14.7 2.6 %gather_fusion.1 = f32[1536,64]{1,0:T(8,128)S(1)} fusion(f32[64,320]{0,1:T(8,128)S(1)} %copy.26, s32[2048]{0:T(1024)S(1)} %pad_clamp_fusion), kind=kCustom, calls=%fused_computation.1.clone | custom fusion | bytes 792576 | tf_op jit(solution)/shard_map/jit(_take)/gather | solution.py:46
  17.3 0.2 copy.27
  17.6 0.4 convolution_bitcast_fusion.5
  18.0 0.2 fusion.18
  18.2 0.1 slice.65
  18.3 0.2 collective-permute-start.3
  18.5 0.5 copy-done.4
  19.0 0.5 collective-permute-done.3
  19.5 0.1 copy.28
  19.6 2.6 %gather_fusion.2 = f32[1536,64]{1,0:T(8,128)S(1)} fusion(f32[64,320]{0,1:T(8,128)S(1)} %copy.28, s32[2048]{0:T(1024)S(1)} %pad_clamp_fusion), kind=kCustom, calls=%fused_computation.2.clone | custom fusion | bytes 792576 | tf_op jit(solution)/shard_map/jit(_take)/gather | solution.py:46
  22.2 0.2 copy.29
  22.5 0.4 convolution_bitcast_fusion.4
  22.9 0.2 fusion.15
  23.1 0.1 slice.67
  23.2 0.2 collective-permute-start.4
  23.4 32.6 %all_gather.10 = f32[8,64,256]{2,1,0:T(8,128)S(1)} all-gather(f32[1,64,256]{2,1,0:T(8,128)S(1)} %convert_element_type.15), channel_id=1, replica_groups=mesh['groups'=2,'tm'=8,'space'=2] {'tm'}, dimensions={0}, use_global_device_ids=true | all-gather | bytes 589824 | tf_op jit(solution)/shard_map/all_gather | solution.py:31
  55.9 0.1 copy.30
  56.1 2.6 %gather_fusion.3 = f32[1536,64]{1,0:T(8,128)S(1)} fusion(f32[64,320]{0,1:T(8,128)S(1)} %copy.30, s32[2048]{0:T(1024)S(1)} %pad_clamp_fusion), kind=kCustom, calls=%fused_computation.3.clone | custom fusion | bytes 792576 | tf_op jit(solution)/shard_map/jit(_take)/gather | solution.py:46
  58.7 0.2 copy.31
  58.9 0.4 convolution_bitcast_fusion.3
  59.3 0.4 copy-done.2
  59.8 0.2 fusion.22
  60.0 31.2 %all-gather = f32[512,256]{1,0:T(8,128)S(1)} all-gather(f32[64,256]{1,0:T(8,128)S(1)} %fusion.22), channel_id=2, replica_groups=mesh['groups'=2,'tm'=8,'space'=2] {'tm'}, dimensions={0}, use_global_device_ids=true | all-gather | bytes 589824 | tf_op jit(solution)/shard_map/all_gather | solution.py:31
  91.2 0.1 slice.69
  91.3 1.2 %collective-permute-done.5 = f32[64,64]{1,0:T(8,128)S(1)} collective-permute-done((f32[64,64]{1,0:T(8,128)S(1)}, f32[64,64]{1,0:T(8,128)S(1)}, u32[]{:S(2)}, u32[]{:S(2)}) %collective-permute-start.5) | collective-permute-done | bytes 16416 | tf_op jit(solution)/shard_map/ppermute | solution.py:20
  92.5 0.1 copy.32
  92.6 2.6 %gather_fusion.4 = f32[1536,64]{1,0:T(8,128)S(1)} fusion(f32[64,320]{0,1:T(8,128)S(1)} %copy.32, s32[2048]{0:T(1024)S(1)} %pad_clamp_fusion), kind=kCustom, calls=%fused_computation.4.clone | custom fusion | bytes 792576 | tf_op jit(solution)/shard_map/jit(_take)/gather | solution.py:46
  95.2 0.2 copy.33
  95.5 0.4 convolution_bitcast_fusion.2
  95.9 0.2 fusion.9
  96.1 0.1 slice.70
  96.2 0.2 collective-permute-start.6
  96.4 1.0 collective-permute-done.6
  97.4 0.1 copy.34
  97.5 2.6 %gather_fusion.5 = f32[1536,64]{1,0:T(8,128)S(1)} fusion(f32[64,320]{0,1:T(8,128)S(1)} %copy.34, s32[2048]{0:T(1024)S(1)} %pad_clamp_fusion), kind=kCustom, calls=%fused_computation.5.clone | custom fusion | bytes 792576 | tf_op jit(solution)/shard_map/jit(_take)/gather | solution.py:46
  100.1 0.2 copy.35
  100.4 0.4 convolution_bitcast_fusion.1
  100.8 0.2 fusion.6
  101.0 0.1 slice.71
  101.1 0.2 collective-permute-start.7
  101.3 1.0 collective-permute-done.7
  102.3 0.1 copy.36
  102.4 2.6 %gather_fusion.6 = f32[1536,64]{1,0:T(8,128)S(1)} fusion(f32[64,320]{0,1:T(8,128)S(1)} %copy.36, s32[2048]{0:T(1024)S(1)} %pad_clamp_fusion), kind=kCustom, calls=%fused_computation.6.clone | custom fusion | bytes 792576 | tf_op jit(solution)/shard_map/jit(_take)/gather | solution.py:46
  105.0 0.2 copy.37
  105.3 0.4 convolution_bitcast_fusion
  105.7 0.2 fusion.3
  105.9 0.7 pad_maximum_fusion
  (31 shorter events, 0.2 us)
Async XLA Ops:
  0.0 12.3 %copy-start = (f32[6,64,64]{2,1,0:T(8,128)S(1)}, f32[6,64,64]{2,1,0:T(8,128)}, u32[]{:S(2)}) copy-start(f32[6,64,64]{2,1,0:T(8,128)} %param.17) | copy-start | bytes 294916
  0.0 5.7 %copy-start.6 = (s32[6,256]{1,0:T(8,128)S(1)}, s32[6,256]{1,0:T(8,128)}, u32[]{:S(2)}) copy-start(s32[6,256]{1,0:T(8,128)} %param.19) | copy-start | bytes 18436
  0.0 7.2 %collective-permute-start = (f32[64,256]{1,0:T(8,128)}, f32[64,256]{1,0:T(8,128)S(1)}, u32[]{:S(2)}, u32[]{:S(2)}) collective-permute-start(f32[64,256]{1,0:T(8,128)} %bitcast.155), channel_id=1, source_target_pairs={{0,2},{2,4},{4,6},{6,8},{8,10},{10,12},{12,14},{1,3},{3,5},{5,7},{... | collective-permute-start | bytes 196616 | tf_op jit(solution)/shard_map/ppermute | solution.py:26
  5.7 3.1 %copy-start.3 = (bf16[4,64,256]{2,1,0:T(8,128)(2,1)S(1)}, bf16[4,64,256]{2,1,0:T(8,128)(2,1)}, u32[]{:S(2)}) copy-start(bf16[4,64,256]{2,1,0:T(8,128)(2,1)} %param.14) | copy-start | bytes 393220
  8.1 0.7 copy-start.7
  8.1 1.2 %collective-permute-start.1 = (f32[64,64]{1,0:T(8,128)S(1)}, f32[64,64]{1,0:T(8,128)S(1)}, u32[]{:S(2)}, u32[]{:S(2)}) collective-permute-start(f32[64,64]{1,0:T(8,128)S(1)} %slice.61), channel_id=1, source_target_pairs={{0,1},{1,0},{2,3},{3,2},{4,5},{5,4},{6,7},{7,6},{8,9},{9,8},{10,11... | collective-permute-start | bytes 49160 | tf_op jit(solution)/shard_map/ppermute | solution.py:20
  12.3 0.8 copy-start.1
  12.3 0.8 copy-start.5
  13.4 1.2 %collective-permute-start.2 = (f32[64,64]{1,0:T(8,128)S(1)}, f32[64,64]{1,0:T(8,128)S(1)}, u32[]{:S(2)}, u32[]{:S(2)}) collective-permute-start(f32[64,64]{1,0:T(8,128)S(1)} %slice.63), channel_id=1, source_target_pairs={{0,1},{1,0},{2,3},{3,2},{4,5},{5,4},{6,7},{7,6},{8,9},{9,8},{10,11... | collective-permute-start | bytes 49160 | tf_op jit(solution)/shard_map/ppermute | solution.py:20
  18.2 0.8 copy-start.4
  18.3 1.2 %collective-permute-start.3 = (f32[64,64]{1,0:T(8,128)S(1)}, f32[64,64]{1,0:T(8,128)S(1)}, u32[]{:S(2)}, u32[]{:S(2)}) collective-permute-start(f32[64,64]{1,0:T(8,128)S(1)} %slice.65), channel_id=1, source_target_pairs={{0,1},{1,0},{2,3},{3,2},{4,5},{5,4},{6,7},{7,6},{8,9},{9,8},{10,11... | collective-permute-start | bytes 49160 | tf_op jit(solution)/shard_map/ppermute | solution.py:20
  23.2 32.7 %collective-permute-start.4 = (f32[64,64]{1,0:T(8,128)S(1)}, f32[64,64]{1,0:T(8,128)S(1)}, u32[]{:S(2)}, u32[]{:S(2)}) collective-permute-start(f32[64,64]{1,0:T(8,128)S(1)} %slice.67), channel_id=1, source_target_pairs={{0,1},{1,0},{2,3},{3,2},{4,5},{5,4},{6,7},{7,6},{8,9},{9,8},{10,11... | collective-permute-start | bytes 49160 | tf_op jit(solution)/shard_map/ppermute | solution.py:20
  58.9 0.8 copy-start.2
  91.3 1.2 %collective-permute-start.5 = (f32[64,64]{1,0:T(8,128)S(1)}, f32[64,64]{1,0:T(8,128)S(1)}, u32[]{:S(2)}, u32[]{:S(2)}) collective-permute-start(f32[64,64]{1,0:T(8,128)S(1)} %slice.69), channel_id=1, source_target_pairs={{0,1},{1,0},{2,3},{3,2},{4,5},{5,4},{6,7},{7,6},{8,9},{9,8},{10,11... | collective-permute-start | bytes 49160 | tf_op jit(solution)/shard_map/ppermute | solution.py:20
  96.2 1.2 %collective-permute-start.6 = (f32[64,64]{1,0:T(8,128)S(1)}, f32[64,64]{1,0:T(8,128)S(1)}, u32[]{:S(2)}, u32[]{:S(2)}) collective-permute-start(f32[64,64]{1,0:T(8,128)S(1)} %slice.70), channel_id=1, source_target_pairs={{0,1},{1,0},{2,3},{3,2},{4,5},{5,4},{6,7},{7,6},{8,9},{9,8},{10,11... | collective-permute-start | bytes 49160 | tf_op jit(solution)/shard_map/ppermute | solution.py:20
  101.1 1.2 %collective-permute-start.7 = (f32[64,64]{1,0:T(8,128)S(1)}, f32[64,64]{1,0:T(8,128)S(1)}, u32[]{:S(2)}, u32[]{:S(2)}) collective-permute-start(f32[64,64]{1,0:T(8,128)S(1)} %slice.71), channel_id=1, source_target_pairs={{0,1},{1,0},{2,3},{3,2},{4,5},{5,4},{6,7},{7,6},{8,9},{9,8},{10,11... | collective-permute-start | bytes 49160 | tf_op jit(solution)/shard_map/ppermute | solution.py:20
where the time goes:
time: 107 us
  blocking collectives  63.8 us (60%)
  local copies, waits for them, and re-layouts  23.1 us (22%)
  waiting for transfers between devices  6.81 us (6%)
  starting transfers between devices  5.86 us (5%)
  matrix products  4.26 us (4%)
  other arithmetic  2.4 us (2%)
    all_gather x2, blocking collectives, carried_in(): gathered = jax.tree.map(lambda a: lax.all_gather(a, axis), part)  63.8 us
    gather x14, local copies, waits for them, and re-layouts, propagate(): nearby = jnp.take(extended, neighbors, axis=1) * weights[None]  19.9 us
    ppermute x7, waiting for transfers between devices, swapped(): return lax.ppermute(block, axis, route)  5.36 us
    ppermute x1, starting transfers between devices, from_behind(): return lax.ppermute(array, axis, pairs)  4.97 us
    dot_general x7, matrix products, propagate(): jnp.einsum('fij,jfe->ie', face_blocks, nearby, precision=highest, preferr...  2.86 us
  transfers between devices with their start and end apart: 8, of which 7 were waited for; matrix products, arithmetic and copies ran while one was open for 1% of the time, Pallas kernels for 0%

commit v1 on v0

v1 whole, which is shorter than its diff:
```python
import functools

import jax
import jax.numpy as jnp
from jax import lax
from jax.experimental import pallas as pl
from jax.experimental.pallas import tpu as pltpu
from jax.sharding import PartitionSpec as P

CF = 4
BND = 64
LANES = 128
MESH = pl.DeviceIdType.MESH


def radices(count):
    out = []
    while count > 1:
        for m in (4, 2, count):
            if count % m == 0:
                out.append(m)
                count //= m
                break
    return out or [1]


def kernel(
    count,
    stages,
    iterate,
    forcing,
    initial,
    self_block,
    face_blocks,
    gain,
    neighbors,
    face_mask,
    decay,
    out,
    start,
    cur,
    source,
    partner_source,
    where_from,
    gains,
    weights,
    high,
    low,
    residual,
    entering,
    rslots,
    dslots,
    core_send,
    core_recv,
    step_send,
    step_recv,
    rsend,
    rrecv,
    dsend,
    drecv,
):
    f32, bf16 = jnp.float32, jnp.bfloat16
    g, t, s = (lax.axis_index(a) for a in ("groups", "tm", "space"))
    other = (g, t, 1 - s)
    rows, width = initial.shape

    digits, strides, stride = [], [], 1
    for m in stages:
        digits.append(lax.rem(t // stride, m))
        strides.append(stride)
        stride *= m

    barrier = pltpu.get_barrier_semaphore()
    pl.semaphore_signal(barrier, inc=1, device_id=other, device_id_type=MESH)
    greeted = 1
    if count > 1:
        for by in (1, count - 1):
            for core in (s, 1 - s):
                there = (g, lax.rem(t + by, count), core)
                pl.semaphore_signal(barrier, inc=1, device_id=there, device_id_type=MESH)
                greeted += 1
        for m, digit, stride in zip(stages, digits, strides):
            for by in range(1, m):
                to = t + (lax.rem(digit + by, m) - digit) * stride
                pl.semaphore_signal(barrier, inc=1, device_id=(g, to, s), device_id_type=MESH)
                greeted += 1

    tables = neighbors[...]
    where_from[0, 0:6, :] = jnp.where(face_mask[...] == 0, -1, tables)
    where_from[0, 6:8, :] = jnp.zeros((2, width), jnp.int32)
    gains[0] = jnp.broadcast_to(gain[...][None, :], (8, width))
    source[...] = forcing[...].astype(f32)
    pl.semaphore_wait(barrier, greeted)

    def to_core(src, dst, i):
        return pltpu.make_async_remote_copy(
            src, dst, core_send.at[i], core_recv.at[i], device_id=other, device_id_type=MESH
        )

    def shift(i):
        core = s if i == 0 else 1 - s
        to = lax.rem(t + 1, count)
        return pltpu.make_async_remote_copy(
            iterate.at[0],
            start.at[i],
            step_send.at[i],
            step_recv.at[i],
            device_id=(g, to, core),
            device_id_type=MESH,
        )

    first_half = to_core(initial, start.at[1], 0)
    table_copy = to_core(where_from.at[0], where_from.at[1], 1)
    gain_copy = to_core(gains.at[0], gains.at[1], 2)
    source_copy = to_core(source.at[pl.ds(0, CF - 1)], partner_source, 3)
    entering_copy = to_core(entering.at[0], entering.at[1], 4)

    if count > 1:

        @pl.when(t < count - 1)
        def _():
            shift(0).start()
            shift(1).start()

    @pl.when(t == 0)
    def _():
        first_half.start()

    table_copy.start()
    gain_copy.start()
    source_copy.start()

    def link(slots, send, recv, i, b):
        digit = digits[i]
        base = sum(stages[:i])
        return pltpu.make_async_remote_copy(
            slots.at[base + digit],
            slots.at[base + digit],
            send.at[base + b],
            recv.at[base + digit],
            device_id=(g, t + (b - digit) * strides[i], s),
            device_id_type=MESH,
        )

    def arrival(slots, send, recv, i, b):
        base = sum(stages[:i])
        return pltpu.make_async_remote_copy(
            slots.at[base + b],
            slots.at[base + b],
            send.at[base + b],
            recv.at[base + b],
            device_id=(g, t, s),
            device_id_type=MESH,
        )

    def each_out(i, act):
        for b in range(stages[i]):
            last = i == len(stages) - 1
            pl.when(b > digits[i] if last else b != digits[i])(functools.partial(act, b))

    def each_in(i, act):
        for b in range(stages[i]):
            last = i == len(stages) - 1
            pl.when(b < digits[i] if last else b != digits[i])(functools.partial(act, b))

    def send(slots, ss, rs, i, value):
        slots[sum(stages[:i]) + digits[i]] = value
        each_out(i, lambda b: link(slots, ss, rs, i, b).start())

    def receive(slots, ss, rs, i):
        each_in(i, lambda b: arrival(slots, ss, rs, i, b).wait_recv())

    damping = decay[0].astype(f32)
    send(dslots, dsend, drecv, 0, damping)

    blocks = jnp.concatenate([self_block[...]] + [face_blocks[f] for f in range(6)], axis=1)
    upper = blocks.astype(bf16)
    weights[0:rows, :] = upper
    weights[rows : 2 * rows, :] = (blocks - upper.astype(f32)).astype(bf16)

    def put(r, cols, value):
        top = value.astype(bf16)
        high[r * rows : (r + 1) * rows, cols] = top
        low[r * rows : (r + 1) * rows, cols] = (value - top.astype(f32)).astype(bf16)

    def advance(field, halves):
        for h in range(halves):
            near = [field[h, :, LANES * i : LANES * (i + 1)] for i in range(width // LANES)]
            far = field[1 - h, :, width - LANES :]
            for i in range(width // LANES):
                cols = slice(h * width + LANES * i, h * width + LANES * (i + 1))
                put(0, cols, near[i])
                for f in range(6):
                    v = where_from[h, f : f + 1, LANES * i : LANES * (i + 1)]
                    lane = lax.bitwise_and(jnp.where(v >= width, v - BND, v), LANES - 1)
                    lane = jnp.broadcast_to(lane, (rows, LANES))
                    v = jnp.broadcast_to(v, (rows, LANES))
                    got = jnp.take_along_axis(far, lane, axis=1)
                    for k in reversed(range(width // LANES)):
                        here = jnp.take_along_axis(near[k], lane, axis=1)
                        got = jnp.where(v < LANES * (k + 1), here, got)
                    put(f + 1, cols, jnp.where(v < 0, 0.0, got))
        n = halves * width
        both = jnp.dot(weights[...], high[:, :n], preferred_element_type=f32)
        rest = jnp.dot(weights[0:rows, :], low[:, :n], preferred_element_type=f32)
        total = both[:rows] + (both[rows:] + rest)
        return [total[:, h * width : (h + 1) * width] * gains[h, 0:1, :] for h in range(halves)]

    if count > 1:

        @pl.when(t > 0)
        def _():
            shift(0).wait_recv()
            shift(1).wait_recv()

    @pl.when(t == 0)
    def _():
        start[0] = initial[...]
        first_half.wait_recv()

    table_copy.wait_recv()
    gain_copy.wait_recv()

    def decay_stage(i, product, before):
        receive(dslots, dsend, drecv, i)
        base = sum(stages[:i])
        lead = jnp.ones((rows, width), f32)
        whole = lead
        for b in range(stages[i]):
            part = dslots[base + b]
            lead = jnp.where(b < digits[i], lead * part, lead)
            whole = whole * part
        return whole, before * lead

    befores = [jnp.ones((rows, width), f32)]
    product = damping
    field = start
    for j in range(CF):
        got = advance(field, 2 if j < CF - 1 else 1)
        if j == 0:
            source_copy.wait_recv()
        if j < CF - 1:
            cur[0] = got[0] + source[j]
            cur[1] = got[1] + partner_source[j]
            field = cur
        if j == 1:
            for i in range(len(stages) - 1):
                product, after = decay_stage(i, product, befores[-1])
                befores.append(after)
                send(dslots, dsend, drecv, i + 1, product)
    local = (got[0] + source[CF - 1]) - iterate[0]
    residual[...] = local

    term = local
    prefix = jnp.zeros((rows, width), f32)
    for i in range(len(stages)):
        send(rslots, rsend, rrecv, i, term)
        base = sum(stages[:i])
        if i == len(stages) - 1:
            receive(dslots, dsend, drecv, i)
        receive(rslots, rsend, rrecv, i)
        carried = jnp.zeros((rows, width), f32)
        whole = carried
        for b in range(stages[i]):
            r, d = rslots[base + b], dslots[base + b]
            carried = jnp.where(b < digits[i], d * carried + r, carried)
            if i < len(stages) - 1:
                whole = d * whole + r
        prefix = prefix + befores[i] * carried
        term = whole
    entering[0] = prefix
    entering_copy.start()
    cur[0] = start[0] + prefix
    out[CF - 1] = iterate[0] + (damping * prefix + residual[...])
    entering_copy.wait_recv()
    cur[1] = start[1] + entering[1]
    for j in range(CF - 1):
        got = advance(cur, 2 if j < CF - 2 else 1)
        out[j] = got[0] + source[j]
        if j < CF - 2:
            cur[0] = out[j]
            cur[1] = got[1] + partner_source[j]

    for copy in (table_copy, gain_copy, source_copy, entering_copy):
        copy.wait_send()

    @pl.when(t == 0)
    def _():
        first_half.wait_send()

    if count > 1:

        @pl.when(t < count - 1)
        def _():
            shift(0).wait_send()
            shift(1).wait_send()

    for i in range(len(stages)):
        each_out(i, lambda b: link(dslots, dsend, drecv, i, b).wait_send())
        each_out(i, lambda b: link(rslots, rsend, rrecv, i, b).wait_send())


def solution(mesh):
    count = mesh.shape["tm"]
    stages = radices(count)
    slots = sum(stages)

    def local(iterate, forcing, initial, *rest):
        rows, width = initial.shape
        f32 = jnp.float32
        vmem = pl.BlockSpec(memory_space=pltpu.VMEM)
        dma = pltpu.SemaphoreType.DMA
        field = (rows, width)
        return pl.pallas_call(
            functools.partial(kernel, count, stages),
            out_shape=jax.ShapeDtypeStruct((CF, rows, width), f32),
            in_specs=[vmem] * 9,
            out_specs=vmem,
            scratch_shapes=[
                pltpu.VMEM((2,) + field, f32),
                pltpu.VMEM((2,) + field, f32),
                pltpu.VMEM((CF,) + field, f32),
                pltpu.VMEM((CF - 1,) + field, f32),
                pltpu.VMEM((2, 8, width), jnp.int32),
                pltpu.VMEM((2, 8, width), f32),
                pltpu.VMEM((2 * rows, 7 * rows), jnp.bfloat16),
                pltpu.VMEM((7 * rows, 2 * width), jnp.bfloat16),
                pltpu.VMEM((7 * rows, 2 * width), jnp.bfloat16),
                pltpu.VMEM(field, f32),
                pltpu.VMEM((2,) + field, f32),
                pltpu.VMEM((slots,) + field, f32),
                pltpu.VMEM((slots,) + field, f32),
                dma((5,)),
                dma((5,)),
                dma((2,)),
                dma((2,)),
                dma((slots,)),
                dma((slots,)),
                dma((slots,)),
                dma((slots,)),
            ],
            compiler_params=pltpu.CompilerParams(
                collective_id=0, has_side_effects=True, vmem_limit_bytes=32 << 20
            ),
        )(iterate, forcing, initial, *rest)

    placed = (
        P(("groups", "tm"), None, "space"),
        P(("groups", "tm"), None, "space"),
        P("groups", "space"),
        P(),
        P(),
        P("space"),
        P(None, "space"),
        P(None, "space"),
        P(("groups", "tm"), None, "space"),
    )
    return jax.shard_map(
        local,
        mesh=mesh,
        in_specs=placed,
        out_specs=P(("groups", "tm"), None, "space"),
        check_vma=False,
    )
```

time: 107 us -> 34.2 us (0.32)
  the two profiles are of different devices: /device:TPU:0 before, /device:TPU:25 now
where the time goes in v1:
time: 34.2 us; the launch traced here: 33.7 us
  Pallas kernels  25.9 us (76%)
  local copies, waits for them, and re-layouts  7.8 us (23%)
    pallas_call x1, Pallas kernels, local(): pl.pallas_call(functools.partial(kernel, count, stages), out_shape=jax.Sh...  25.9 us
    unnamed x19, local copies, waits for them, and re-layouts  7.8 us

profile of v1, /device:TPU:25, one launch (start us, length us, event | category | flops | bytes accessed | tf_op | source)
XLA Modules:
  0.0 33.7 jit_solution(12706082496828074277)
XLA Ops:
  0.0 0.0 copy-start
  0.0 0.9 %copy-done = f32[6,64,64]{2,1,0:T(8,128)S(1)} copy-done((f32[6,64,64]{2,1,0:T(8,128)S(1)}, f32[6,64,64]{2,1,0:T(8,128)}, u32[]{:S(2)}) %copy-start) | copy-done | bytes 98328
  0.9 0.0 copy-start.1
  0.9 0.9 %copy-done.1 = bf16[4,64,256]{2,1,0:T(8,128)(2,1)S(1)} copy-done((bf16[4,64,256]{2,1,0:T(8,128)(2,1)S(1)}, bf16[4,64,256]{2,1,0:T(8,128)(2,1)}, u32[]{:S(2)}) %copy-start.1) | copy-done | bytes 131096
  1.8 0.0 copy-start.2
  1.8 0.8 %copy-done.2 = f32[1,64,256]{2,1,0:T(8,128)S(1)} copy-done((f32[1,64,256]{2,1,0:T(8,128)S(1)}, f32[1,64,256]{2,1,0:T(8,128)}, u32[]{:S(2)}) %copy-start.2) | copy-done | bytes 65560
  2.7 0.0 copy-start.3
  2.7 0.8 %copy-done.3 = f32[64,256]{1,0:T(8,128)S(1)} copy-done((f32[64,256]{1,0:T(8,128)S(1)}, f32[64,256]{1,0:T(8,128)}, u32[]{:S(2)}) %copy-start.3) | copy-done | bytes 65560
  3.5 0.0 copy-start.4
  3.5 0.8 %copy-done.4 = f32[64,64]{1,0:T(8,128)S(1)} copy-done((f32[64,64]{1,0:T(8,128)S(1)}, f32[64,64]{1,0:T(8,128)}, u32[]{:S(2)}) %copy-start.4) | copy-done | bytes 16408
  4.3 0.0 copy-start.5
  4.3 0.8 %copy-done.5 = bf16[1,64,256]{2,1,0:T(8,128)(2,1)S(1)} copy-done((bf16[1,64,256]{2,1,0:T(8,128)(2,1)S(1)}, bf16[1,64,256]{2,1,0:T(8,128)(2,1)}, u32[]{:S(2)}) %copy-start.5) | copy-done | bytes 32792
  5.0 0.0 copy-start.6
  5.0 0.7 %copy-done.6 = s32[6,256]{1,0:T(8,128)S(1)} copy-done((s32[6,256]{1,0:T(8,128)S(1)}, s32[6,256]{1,0:T(8,128)}, u32[]{:S(2)}) %copy-start.6) | copy-done | bytes 6168
  5.7 0.0 copy-start.7
  5.7 0.7 %copy-done.7 = s32[6,256]{1,0:T(8,128)S(1)} copy-done((s32[6,256]{1,0:T(8,128)S(1)}, s32[6,256]{1,0:T(8,128)}, u32[]{:S(2)}) %copy-start.7) | copy-done | bytes 6168
  6.4 0.0 copy-start.8
  6.4 0.7 %copy-done.8 = f32[256]{0:T(256)S(1)} copy-done((f32[256]{0:T(256)S(1)}, f32[256]{0:T(256)}, u32[]{:S(2)}) %copy-start.8) | copy-done | bytes 1048
  7.1 25.9 %shard_map.91 = f32[4,64,256]{2,1,0:T(8,128)S(1)} custom-call(f32[1,64,256]{2,1,0:T(8,128)S(1)} %copy-done.2, bf16[4,64,256]{2,1,0:T(8,128)(2,1)S(1)} %copy-done.1, f32[64,256]{1,0:T(8,128)S(1)} %copy-done.3, f32[64,64]{1,0:T(8,128)S(1)} %copy-done.4, f32[6,64,64]{2,1,0:T(8,128)S(1)} %copy-done, f32[256]{0:T(256)S(1)} %copy-done.8, s32[6,256]{1,0:T(8,128)S(1)} %copy-done.6, ...), custom_call_target="tpu_custom_call" | custom-call | tf_op jit(solution)/shard_map/pallas_call | solution.py:314
  33.0 0.7 %copy.11 = f32[4,64,256]{2,1,0:T(8,128)} copy(f32[4,64,256]{2,1,0:T(8,128)S(1)} %shard_map.91) | data formatting | bytes 524288
Async XLA Ops:
  0.0 0.9 %copy-start = (f32[6,64,64]{2,1,0:T(8,128)S(1)}, f32[6,64,64]{2,1,0:T(8,128)}, u32[]{:S(2)}) copy-start(f32[6,64,64]{2,1,0:T(8,128)} %face_blocks.1) | copy-start | bytes 294916
  0.9 0.9 %copy-start.1 = (bf16[4,64,256]{2,1,0:T(8,128)(2,1)S(1)}, bf16[4,64,256]{2,1,0:T(8,128)(2,1)}, u32[]{:S(2)}) copy-start(bf16[4,64,256]{2,1,0:T(8,128)(2,1)} %forcing.1) | copy-start | bytes 393220
  1.8 0.8 %copy-start.2 = (f32[1,64,256]{2,1,0:T(8,128)S(1)}, f32[1,64,256]{2,1,0:T(8,128)}, u32[]{:S(2)}) copy-start(f32[1,64,256]{2,1,0:T(8,128)} %iterate.1) | copy-start | bytes 196612
  2.7 0.8 %copy-start.3 = (f32[64,256]{1,0:T(8,128)S(1)}, f32[64,256]{1,0:T(8,128)}, u32[]{:S(2)}) copy-start(f32[64,256]{1,0:T(8,128)} %initial.1) | copy-start | bytes 196612
  3.5 0.8 %copy-start.4 = (f32[64,64]{1,0:T(8,128)S(1)}, f32[64,64]{1,0:T(8,128)}, u32[]{:S(2)}) copy-start(f32[64,64]{1,0:T(8,128)} %self_block.1) | copy-start | bytes 49156
  4.3 0.8 %copy-start.5 = (bf16[1,64,256]{2,1,0:T(8,128)(2,1)S(1)}, bf16[1,64,256]{2,1,0:T(8,128)(2,1)}, u32[]{:S(2)}) copy-start(bf16[1,64,256]{2,1,0:T(8,128)(2,1)} %decay.1) | copy-start | bytes 98308
  5.0 0.7 %copy-start.6 = (s32[6,256]{1,0:T(8,128)S(1)}, s32[6,256]{1,0:T(8,128)}, u32[]{:S(2)}) copy-start(s32[6,256]{1,0:T(8,128)} %neighbors.1) | copy-start | bytes 18436
  5.7 0.7 %copy-start.7 = (s32[6,256]{1,0:T(8,128)S(1)}, s32[6,256]{1,0:T(8,128)}, u32[]{:S(2)}) copy-start(s32[6,256]{1,0:T(8,128)} %face_mask.1) | copy-start | bytes 18436
  6.4 0.7 %copy-start.8 = (f32[256]{0:T(256)S(1)}, f32[256]{0:T(256)}, u32[]{:S(2)}) copy-start(f32[256]{0:T(256)} %gain.1) | copy-start | bytes 3076

commit v2 on v1

--- a/solution.py
+++ b/solution.py
@@ -27,16 +27,24 @@
 def kernel(
     count,
     stages,
+    iterate_at,
+    forcing_at,
+    initial_at,
+    self_at,
+    face_at,
+    gain_at,
+    neighbors_at,
+    face_mask_at,
+    decay_at,
+    out,
     iterate,
     forcing,
-    initial,
     self_block,
     face_blocks,
     gain,
     neighbors,
     face_mask,
     decay,
-    out,
     start,
     cur,
     source,
@@ -58,11 +66,34 @@
     rrecv,
     dsend,
     drecv,
+    loaded,
 ):
     f32, bf16 = jnp.float32, jnp.bfloat16
     g, t, s = (lax.axis_index(a) for a in ("groups", "tm", "space"))
     other = (g, t, 1 - s)
-    rows, width = initial.shape
+    rows, width = initial_at.shape
+
+    loads = {}
+    for i, (name, src, dst) in enumerate(
+        (
+            ("neighbors", neighbors_at, neighbors),
+            ("face_mask", face_mask_at, face_mask),
+            ("gain", gain_at, gain),
+            ("decay", decay_at, decay),
+            ("forcing", forcing_at, forcing),
+            ("self_block", self_at, self_block),
+            ("face_blocks", face_at, face_blocks),
+            ("iterate", iterate_at, iterate),
+            ("initial", initial_at, start.at[0]),
+        )
+    ):
+        loads[name] = pltpu.make_async_copy(src, dst, loaded.at[i])
+        if name != "initial":
+            loads[name].start()
+
+    @pl.when(t == 0)
+    def _():
+        loads["initial"].start()
 
     digits, strides, stride = [], [], 1
     for m in stages:
@@ -85,13 +116,6 @@
                 pl.semaphore_signal(barrier, inc=1, device_id=(g, to, s), device_id_type=MESH)
                 greeted += 1
 
-    tables = neighbors[...]
-    where_from[0, 0:6, :] = jnp.where(face_mask[...] == 0, -1, tables)
-    where_from[0, 6:8, :] = jnp.zeros((2, width), jnp.int32)
-    gains[0] = jnp.broadcast_to(gain[...][None, :], (8, width))
-    source[...] = forcing[...].astype(f32)
-    pl.semaphore_wait(barrier, greeted)
-
     def to_core(src, dst, i):
         return pltpu.make_async_remote_copy(
             src, dst, core_send.at[i], core_recv.at[i], device_id=other, device_id_type=MESH
@@ -101,7 +125,7 @@
         core = s if i == 0 else 1 - s
         to = lax.rem(t + 1, count)
         return pltpu.make_async_remote_copy(
-            iterate.at[0],
+            iterate_at.at[0],
             start.at[i],
             step_send.at[i],
             step_recv.at[i],
@@ -109,12 +133,13 @@
             device_id_type=MESH,
         )
 
-    first_half = to_core(initial, start.at[1], 0)
+    first_half = to_core(initial_at, start.at[1], 0)
     table_copy = to_core(where_from.at[0], where_from.at[1], 1)
     gain_copy = to_core(gains.at[0], gains.at[1], 2)
     source_copy = to_core(source.at[pl.ds(0, CF - 1)], partner_source, 3)
     entering_copy = to_core(entering.at[0], entering.at[1], 4)
 
+    pl.semaphore_wait(barrier, greeted)
     if count > 1:
 
         @pl.when(t < count - 1)
@@ -126,9 +151,13 @@
     def _():
         first_half.start()
 
+    for name in ("neighbors", "face_mask", "gain"):
+        loads[name].wait()
+    where_from[0, 0:6, :] = jnp.where(face_mask[...] == 0, -1, neighbors[...])
+    where_from[0, 6:8, :] = jnp.zeros((2, width), jnp.int32)
+    gains[0] = jnp.broadcast_to(gain[...][None, :], (8, width))
     table_copy.start()
     gain_copy.start()
-    source_copy.start()
 
     def link(slots, send, recv, i, b):
         digit = digits[i]
@@ -170,8 +199,14 @@
     def receive(slots, ss, rs, i):
         each_in(i, lambda b: arrival(slots, ss, rs, i, b).wait_recv())
 
+    loads["decay"].wait()
     damping = decay[0].astype(f32)
     send(dslots, dsend, drecv, 0, damping)
+    loads["forcing"].wait()
+    source[...] = forcing[...].astype(f32)
+    source_copy.start()
+    for name in ("self_block", "face_blocks", "iterate"):
+        loads[name].wait()
 
     blocks = jnp.concatenate([self_block[...]] + [face_blocks[f] for f in range(6)], axis=1)
     upper = blocks.astype(bf16)
@@ -215,7 +250,7 @@
 
     @pl.when(t == 0)
     def _():
-        start[0] = initial[...]
+        loads["initial"].wait()
         first_half.wait_recv()
 
     table_copy.wait_recv()
@@ -309,14 +344,17 @@
         rows, width = initial.shape
         f32 = jnp.float32
         vmem = pl.BlockSpec(memory_space=pltpu.VMEM)
+        hbm = pl.BlockSpec(memory_space=pltpu.HBM)
+        operands = (iterate, forcing) + rest
         dma = pltpu.SemaphoreType.DMA
         field = (rows, width)
         return pl.pallas_call(
             functools.partial(kernel, count, stages),
             out_shape=jax.ShapeDtypeStruct((CF, rows, width), f32),
-            in_specs=[vmem] * 9,
+            in_specs=[hbm] * 9,
             out_specs=vmem,
-            scratch_shapes=[
+            scratch_shapes=[pltpu.VMEM(a.shape, a.dtype) for a in operands]
+            + [
                 pltpu.VMEM((2,) + field, f32),
                 pltpu.VMEM((2,) + field, f32),
                 pltpu.VMEM((CF,) + field, f32),
@@ -338,9 +376,10 @@
                 dma((slots,)),
                 dma((slots,)),
                 dma((slots,)),
+                dma((9,)),
             ],
             compiler_params=pltpu.CompilerParams(
-                collective_id=0, has_side_effects=True, vmem_limit_bytes=32 << 20
+                collective_id=0, has_side_effects=True
             ),
         )(iterate, forcing, initial, *rest)
 

time: 34.2 us -> 28.7 us (0.84); the launches traced: 33.7 us -> 28.5 us
  local copies, waits for them, and re-layouts: 7.8 us -> 1.67 us
  Pallas kernels: 25.9 us -> 26.9 us
    unnamed x19 -> x1, local copies, waits for them, and re-layouts: 7.8 us -> 1.67 us
    pallas_call x1, Pallas kernels: 25.9 us -> 26.9 us  [local(): pl.pallas_call(functools.partial(kernel, count, stages), out_shape=jax.Sh...]
where the time goes in v2:
time: 28.7 us; the launch traced here: 28.5 us
  Pallas kernels  26.9 us (94%)
  local copies, waits for them, and re-layouts  1.67 us (6%)
    pallas_call x1, Pallas kernels, local(): pl.pallas_call(functools.partial(kernel, count, stages), out_shape=jax.Sh...  26.9 us
    unnamed x1, local copies, waits for them, and re-layouts  1.67 us

profile of v2, /device:TPU:25, one launch (start us, length us, event | category | flops | bytes accessed | tf_op | source)
XLA Modules:
  0.0 28.5 jit_solution(4836822888768333328)
XLA Ops:
  0.0 26.9 %shard_map.91 = f32[4,64,256]{2,1,0:T(8,128)} custom-call(f32[1,64,256]{2,1,0:T(8,128)} %iterate_at.1, bf16[4,64,256]{2,1,0:T(8,128)(2,1)} %forcing_at.1, f32[64,256]{1,0:T(8,128)} %initial_at.1, f32[64,64]{1,0:T(8,128)} %self_at.1, f32[6,64,64]{2,1,0:T(8,128)} %face_at.1, f32[256]{0:T(256)} %gain_at.1, s32[6,256]{1,0:T(8,128)} %neighbors_at.1, ...), custom_call_target="tpu_custom_call" | custom-call | tf_op jit(solution)/shard_map/pallas_call | solution.py:351
  26.9 1.7 %copy.11 = f32[4,64,256]{2,1,0:T(8,128)} copy(f32[4,64,256]{2,1,0:T(8,128)} %shard_map.91) | data formatting | bytes 524288

commit v3 on v2

--- a/solution.py
+++ b/solution.py
@@ -36,7 +36,7 @@
     neighbors_at,
     face_mask_at,
     decay_at,
-    out,
+    out_at,
     iterate,
     forcing,
     self_block,
@@ -67,6 +67,8 @@
     dsend,
     drecv,
     loaded,
+    out,
+    stored,
 ):
     f32, bf16 = jnp.float32, jnp.bfloat16
     g, t, s = (lax.axis_index(a) for a in ("groups", "tm", "space"))
@@ -132,6 +134,9 @@
             device_id=(g, to, core),
             device_id_type=MESH,
         )
+
+    def store(j):
+        return pltpu.make_async_copy(out.at[j], out_at.at[j], stored.at[j])
 
     first_half = to_core(initial_at, start.at[1], 0)
     table_copy = to_core(where_from.at[0], where_from.at[1], 1)
@@ -286,36 +291,60 @@
     local = (got[0] + source[CF - 1]) - iterate[0]
     residual[...] = local
 
-    term = local
-    prefix = jnp.zeros((rows, width), f32)
+    half = rows // 2
+    parts = [slice(0, half), slice(half, rows)]
+
+    def part_link(i, b, c, arriving):
+        base = sum(stages[:i])
+        own = b if arriving else digits[i]
+        ref = rslots.at[base + own, parts[c]]
+        to = t if arriving else t + (b - digits[i]) * strides[i]
+        return pltpu.make_async_remote_copy(
+            ref, ref, rsend.at[base + b, c], rrecv.at[base + own, c],
+            device_id=(g, to, s), device_id_type=MESH,
+        )
+
+    def send_part(i, c, value):
+        rslots[sum(stages[:i]) + digits[i], parts[c]] = value
+        each_out(i, lambda b: part_link(i, b, c, False).start())
+
+    for c in range(2):
+        send_part(0, c, local[parts[c]])
+    prefixes = [jnp.zeros((half, width), f32)] * 2
     for i in range(len(stages)):
-        send(rslots, rsend, rrecv, i, term)
         base = sum(stages[:i])
         if i == len(stages) - 1:
             receive(dslots, dsend, drecv, i)
-        receive(rslots, rsend, rrecv, i)
-        carried = jnp.zeros((rows, width), f32)
-        whole = carried
-        for b in range(stages[i]):
-            r, d = rslots[base + b], dslots[base + b]
-            carried = jnp.where(b < digits[i], d * carried + r, carried)
+        for c in range(2):
+            each_in(i, lambda b: part_link(i, b, c, True).wait_recv())
+            carried = jnp.zeros((half, width), f32)
+            whole = carried
+            for b in range(stages[i]):
+                r, d = rslots[base + b, parts[c]], dslots[base + b, parts[c]]
+                carried = jnp.where(b < digits[i], d * carried + r, carried)
+                if i < len(stages) - 1:
+                    whole = d * whole + r
             if i < len(stages) - 1:
-                whole = d * whole + r
-        prefix = prefix + befores[i] * carried
-        term = whole
+                send_part(i + 1, c, whole)
+            prefixes[c] = prefixes[c] + befores[i][parts[c]] * carried
+    prefix = jnp.concatenate(prefixes, axis=0)
     entering[0] = prefix
     entering_copy.start()
     cur[0] = start[0] + prefix
     out[CF - 1] = iterate[0] + (damping * prefix + residual[...])
+    store(CF - 1).start()
     entering_copy.wait_recv()
     cur[1] = start[1] + entering[1]
     for j in range(CF - 1):
         got = advance(cur, 2 if j < CF - 2 else 1)
         out[j] = got[0] + source[j]
+        store(j).start()
         if j < CF - 2:
             cur[0] = out[j]
             cur[1] = got[1] + partner_source[j]
 
+    for j in range(CF):
+        store(j).wait()
     for copy in (table_copy, gain_copy, source_copy, entering_copy):
         copy.wait_send()
 
@@ -332,7 +361,8 @@
 
     for i in range(len(stages)):
         each_out(i, lambda b: link(dslots, dsend, drecv, i, b).wait_send())
-        each_out(i, lambda b: link(rslots, rsend, rrecv, i, b).wait_send())
+        for c in range(2):
+            each_out(i, lambda b: part_link(i, b, c, False).wait_send())
 
 
 def solution(mesh):
@@ -343,7 +373,6 @@
     def local(iterate, forcing, initial, *rest):
         rows, width = initial.shape
         f32 = jnp.float32
-        vmem = pl.BlockSpec(memory_space=pltpu.VMEM)
         hbm = pl.BlockSpec(memory_space=pltpu.HBM)
         operands = (iterate, forcing) + rest
         dma = pltpu.SemaphoreType.DMA
@@ -352,7 +381,7 @@
             functools.partial(kernel, count, stages),
             out_shape=jax.ShapeDtypeStruct((CF, rows, width), f32),
             in_specs=[hbm] * 9,
-            out_specs=vmem,
+            out_specs=hbm,
             scratch_shapes=[pltpu.VMEM(a.shape, a.dtype) for a in operands]
             + [
                 pltpu.VMEM((2,) + field, f32),
@@ -372,11 +401,13 @@
                 dma((5,)),
                 dma((2,)),
                 dma((2,)),
-                dma((slots,)),
-                dma((slots,)),
+                dma((slots, 2)),
+                dma((slots, 2)),
                 dma((slots,)),
                 dma((slots,)),
                 dma((9,)),
+                pltpu.VMEM((CF,) + field, f32),
+                dma((CF,)),
             ],
             compiler_params=pltpu.CompilerParams(
                 collective_id=0, has_side_effects=True

time: 28.7 us -> 28.2 us (0.983)
  Pallas kernels: 26.9 us -> 26.4 us
    pallas_call x1, Pallas kernels: 26.9 us -> 26.4 us  [local(): pl.pallas_call(functools.partial(kernel, count, stages), out_shape=jax.Sh...]
where the time goes in v3:
time: 28.2 us; the launch traced here: 28 us
  Pallas kernels  26.4 us (94%)
  local copies, waits for them, and re-layouts  1.67 us (6%)
    pallas_call x1, Pallas kernels, local(): pl.pallas_call(functools.partial(kernel, count, stages), out_shape=jax.Sh...  26.4 us
    unnamed x1, local copies, waits for them, and re-layouts  1.67 us

profile of v3, /device:TPU:25, one launch (start us, length us, event | category | flops | bytes accessed | tf_op | source)
XLA Modules:
  0.0 28.0 jit_solution(15942517090428253613)
XLA Ops:
  0.0 26.4 %shard_map.91 = f32[4,64,256]{2,1,0:T(8,128)} custom-call(f32[1,64,256]{2,1,0:T(8,128)} %iterate_at.1, bf16[4,64,256]{2,1,0:T(8,128)(2,1)} %forcing_at.1, f32[64,256]{1,0:T(8,128)} %initial_at.1, f32[64,64]{1,0:T(8,128)} %self_at.1, f32[6,64,64]{2,1,0:T(8,128)} %face_at.1, f32[256]{0:T(256)} %gain_at.1, s32[6,256]{1,0:T(8,128)} %neighbors_at.1, ...), custom_call_target="tpu_custom_call" | custom-call | tf_op jit(solution)/shard_map/pallas_call | solution.py:380
  26.4 1.7 %copy.11 = f32[4,64,256]{2,1,0:T(8,128)} copy(f32[4,64,256]{2,1,0:T(8,128)} %shard_map.91) | data formatting | bytes 524288
